TPU v7x, 128 devices: a whole 4x4x4 slice. The times are simulated.
128 devices in a mesh: row: 8 (over y, core), col: 16 (over z, x).
Axes of the slice: x: 4, y: 4, z: 4, core: 2. Of those that a mesh axis runs over, the one named last changes fastest.
Arguments:
- block_x: float32 [64, 98304], P(None, ('row', 'col')), may hold values from -6 to 6
- block_p: float32 [64, 98304], P(None, ('row', 'col')), may hold values from -6 to 6
- tile_rows: int32 [8, 16, 576], P('row', 'col'), may hold values from 0 to 95, as said below
- tile_cols: int32 [8, 16, 576], P('row', 'col'), may hold values from 0 to 47, as said below
- tile_count: int32 [8, 16], P('row', 'col'), may hold values from 1 to 576, as said below
- tile_vals: bfloat16 [8, 16, 576, 128, 128], P('row', 'col'), may hold values from -0.125 to 0.125
Outputs:
- residual: float32 [64, 98304], P(None, ('row', 'col'))
- image_r: float32 [64, 98304], P(None, ('row', 'col'))
- gram_a: float32 [192, 192], replicated
- gram_b: float32 [192, 192], replicated
Inputs may be any that keep to these rules, and one draw needn't show every extreme that they name: `tile_rows`: within one grid cell the live slots name distinct tiles, all with i <= j; slots at and beyond the cell's count are ignored. `tile_cols`: paired with tile_rows slot by slot. `tile_count`: some grid cell is full in every draw.
All inputs are finite; a program needn't handle non-finite values.
Results may differ from a plain program's by a relative error of at most 0.0035.
Values may be sent and summed in bfloat16 or wider, within the bound.
A program may use at most 128 MiB of HBM per device.

v0:
```python
import math
import jax
import jax.numpy as jnp
from jax import lax
from jax.sharding import PartitionSpec as P


def apply_graph(vectors, tile_rows, tile_cols, live_count, tile_vals):
    vec_width = vectors.shape[0]
    tile_size = tile_vals.shape[-1]
    row_range = lax.all_gather(vectors, "col", axis=1, tiled=True)
    col_group = lax.all_gather(vectors, "row", axis=1, tiled=True)
    row_blocks = row_range.reshape(vec_width, -1, tile_size)
    col_blocks = col_group.reshape(vec_width, -1, tile_size)
    group_size = math.gcd(tile_vals.shape[0], 64)
    offsets = jnp.arange(group_size, dtype=jnp.int32)
    turn_count = (live_count + group_size - 1) // group_size

    def slot_group(turn_index):
        first_slot = turn_index * group_size
        row_index = lax.dynamic_slice_in_dim(tile_rows, first_slot, group_size)
        col_index = lax.dynamic_slice_in_dim(tile_cols, first_slot, group_size)
        values = lax.dynamic_slice_in_dim(tile_vals, first_slot, group_size, 0)
        live_slots = first_slot + offsets < live_count
        return (row_index, col_index, values, live_slots)

    def turn(turn_index, totals):
        row_totals, col_totals = totals
        row_index, col_index, values, live_slots = slot_group(turn_index)
        values = jnp.where(live_slots[:, None, None], values, jnp.zeros_like(values))
        col_inputs = jnp.take(col_blocks, col_index, axis=1)
        row_inputs = jnp.take(row_blocks, row_index, axis=1)
        forward = jnp.einsum("wgb,gab->wga", col_inputs, values, preferred_element_type=jnp.float32)
        backward = jnp.einsum(
            "wga,gab->wgb", row_inputs, values, preferred_element_type=jnp.float32
        )
        return (row_totals.at[:, row_index].add(forward), col_totals.at[:, col_index].add(backward))

    start_rows = jnp.zeros(row_blocks.shape, jnp.float32)
    start_cols = jnp.zeros(col_blocks.shape, jnp.float32)
    row_totals, col_totals = lax.fori_loop(0, turn_count, turn, (start_rows, start_cols))
    own_rows = lax.psum_scatter(
        row_totals.reshape(vec_width, -1), "col", scatter_dimension=1, tiled=True
    )
    own_cols = lax.psum_scatter(
        col_totals.reshape(vec_width, -1), "row", scatter_dimension=1, tiled=True
    )
    return own_rows + own_cols


def per_device(block_x, block_p, tile_rows, tile_cols, tile_count, tile_vals):
    highest = lax.Precision.HIGHEST
    width_k = block_x.shape[0]
    node_count = block_x.shape[1] * lax.axis_size("row") * lax.axis_size("col")
    slot_rows = tile_rows[0, 0]
    slot_cols = tile_cols[0, 0]
    live_count = tile_count[0, 0]
    slot_vals = tile_vals[0, 0]

    def product(left, right):
        return (
            jnp.dot(left, right.T, precision=highest, preferred_element_type=jnp.float32)
            / node_count
        )

    gram_x = lax.psum(product(block_x, block_x), ("row", "col"))
    cholesky_factor = jnp.linalg.cholesky(gram_x)
    orthonormal = lax.linalg.triangular_solve(cholesky_factor, block_x, left_side=True, lower=True)
    ortho_low = orthonormal.astype(jnp.bfloat16)
    dir_low = block_p.astype(jnp.bfloat16)
    both_images = apply_graph(
        jnp.concatenate([ortho_low, dir_low], axis=0), slot_rows, slot_cols, live_count, slot_vals
    )
    image_x = both_images[:width_k]
    image_p = both_images[width_k:]
    rayleigh = lax.psum(product(orthonormal, image_x), ("row", "col"))
    residual = image_x - jnp.dot(
        rayleigh.T, orthonormal, precision=highest, preferred_element_type=jnp.float32
    )
    residual_low = residual.astype(jnp.bfloat16)
    image_r = apply_graph(residual_low, slot_rows, slot_cols, live_count, slot_vals)
    basis = jnp.concatenate([orthonormal, residual, block_p], axis=0)
    images = jnp.concatenate([image_x, image_r, image_p], axis=0)
    gram_a, gram_b = lax.psum((product(basis, images), product(basis, basis)), ("row", "col"))
    return (residual, image_r, gram_a, gram_b)


def solution(mesh):
    in_specs = (
        P(None, ("row", "col")),
        P(None, ("row", "col")),
        P("row", "col", None),
        P("row", "col", None),
        P("row", "col"),
        P("row", "col", None, None, None),
    )
    out_specs = (P(None, ("row", "col")), P(None, ("row", "col")), P(), P())
    return jax.shard_map(
        per_device, mesh=mesh, in_specs=in_specs, out_specs=out_specs, check_vma=False
    )
```

profile of v0, /device:TPU:1, one launch (start us, length us, event | category | flops | bytes accessed | tf_op | source)
XLA Modules:
  0.0 1301.9 jit_solution(9293041823528149920)
XLA Ops:
  8.4 68.9 %psum.28 = f32[64,64]{0,1:T(8,128)S(1)} all-reduce(f32[64,64]{0,1:T(8,128)S(1)} %convolution_multiply_fusion.3), channel_id=1, replica_groups=mesh['row'=8,'col'=16] {'row','col'}, use_global_device_ids=true, to_apply=%region_0.0 | all-reduce | flops 4096 | bytes 32768 | tf_op jit(solution)/shard_map/psum | solution.py:66
  93.1 19.8 %all-gather.4.cloned.1.call-done = bf16[128,6144]{1,0:T(8,128)(2,1)} async-done(((bf16[128,768]{1,0:T(8,128)(2,1)}), bf16[128,6144]{1,0:T(8,128)(2,1)}) %all-gather.4.cloned.1.call-update) | async-done | bytes 1572880 | tf_op jit(solution)/shard_map/all_gather | solution.py:12
  115.9 47.5 %all-gather.6.cloned.1.call-done = bf16[128,12288]{1,0:T(8,128)(2,1)} async-done(((bf16[128,768]{1,0:T(8,128)(2,1)}), bf16[128,12288]{1,0:T(8,128)(2,1)}) %all-gather.6.cloned.1.call-update) | async-done | bytes 3145744 | tf_op jit(solution)/shard_map/all_gather | solution.py:11
  171.6 290.6 %while.26 = (s32[]{:T(128)}, f32[128,96,128]{2,0,1:T(8,128)}, f32[128,48,128]{2,0,1:T(8,128)S(1)}, s32[]{:T(128)}, s32[576]{0:T(1024)S(1)}, /*index=5*/s32[]{:T(...) while((s32[]{:T(128)}, f32[128,96,128]{2,0,1:T(8,128)}, ...), condition=%wide.region_6.7_spmd.clone, body=%wide.region_3.6_spmd.clone.sunk | while | flops 543165312 | bytes 50343056 | solution.py:41
  181.7 13.6 %scatter_fusion = f32[128,96,128]{2,0,1:T(8,128)} fusion(f32[128,96,128]{2,0,1:T(8,128)} %get-tuple-element.407, s32[64]{0:T(128)S(1)} %get-tuple-element.374, f32[64,128,128]{2,1,0:T(8,128)} %fusion.80), kind=kCustom, calls=%fused_computation.4.clone.clone.1 | custom fusion | flops 1048576 | bytes 12583168 | tf_op jit(solution)/shard_map/while/body/scatter-add | solution.py:37
  223.2 13.6 %scatter_fusion = f32[128,96,128]{2,0,1:T(8,128)} fusion(f32[128,96,128]{2,0,1:T(8,128)} %get-tuple-element.407, s32[64]{0:T(128)S(1)} %get-tuple-element.374, f32[64,128,128]{2,1,0:T(8,128)} %fusion.80), kind=kCustom, calls=%fused_computation.4.clone.clone.1 | custom fusion | flops 1048576 | bytes 12583168 | tf_op jit(solution)/shard_map/while/body/scatter-add | solution.py:37
  264.8 13.6 %scatter_fusion = f32[128,96,128]{2,0,1:T(8,128)} fusion(f32[128,96,128]{2,0,1:T(8,128)} %get-tuple-element.407, s32[64]{0:T(128)S(1)} %get-tuple-element.374, f32[64,128,128]{2,1,0:T(8,128)} %fusion.80), kind=kCustom, calls=%fused_computation.4.clone.clone.1 | custom fusion | flops 1048576 | bytes 12583168 | tf_op jit(solution)/shard_map/while/body/scatter-add | solution.py:37
  306.3 13.5 %scatter_fusion = f32[128,96,128]{2,0,1:T(8,128)} fusion(f32[128,96,128]{2,0,1:T(8,128)} %get-tuple-element.407, s32[64]{0:T(128)S(1)} %get-tuple-element.374, f32[64,128,128]{2,1,0:T(8,128)} %fusion.80), kind=kCustom, calls=%fused_computation.4.clone.clone.1 | custom fusion | flops 1048576 | bytes 12583168 | tf_op jit(solution)/shard_map/while/body/scatter-add | solution.py:37
  347.7 13.6 %scatter_fusion = f32[128,96,128]{2,0,1:T(8,128)} fusion(f32[128,96,128]{2,0,1:T(8,128)} %get-tuple-element.407, s32[64]{0:T(128)S(1)} %get-tuple-element.374, f32[64,128,128]{2,1,0:T(8,128)} %fusion.80), kind=kCustom, calls=%fused_computation.4.clone.clone.1 | custom fusion | flops 1048576 | bytes 12583168 | tf_op jit(solution)/shard_map/while/body/scatter-add | solution.py:37
  389.2 13.6 %scatter_fusion = f32[128,96,128]{2,0,1:T(8,128)} fusion(f32[128,96,128]{2,0,1:T(8,128)} %get-tuple-element.407, s32[64]{0:T(128)S(1)} %get-tuple-element.374, f32[64,128,128]{2,1,0:T(8,128)} %fusion.80), kind=kCustom, calls=%fused_computation.4.clone.clone.1 | custom fusion | flops 1048576 | bytes 12583168 | tf_op jit(solution)/shard_map/while/body/scatter-add | solution.py:37
  430.7 13.6 %scatter_fusion = f32[128,96,128]{2,0,1:T(8,128)} fusion(f32[128,96,128]{2,0,1:T(8,128)} %get-tuple-element.407, s32[64]{0:T(128)S(1)} %get-tuple-element.374, f32[64,128,128]{2,1,0:T(8,128)} %fusion.80), kind=kCustom, calls=%fused_computation.4.clone.clone.1 | custom fusion | flops 1048576 | bytes 12583168 | tf_op jit(solution)/shard_map/while/body/scatter-add | solution.py:37
  470.4 106.4 %reduce-scatter.7.cloned.1.call-done = f32[128,768]{1,0:T(8,128)} async-done(((f32[128,6144]{1,0:T(8,128)}), f32[128,768]{1,0:T(8,128)}) %reduce-scatter.7.cloned.1.call-update) | async-done | bytes 393232 | tf_op jit(solution)/shard_map/reduce_scatter | solution.py:45
  576.8 85.4 %reduce-scatter.5.cloned.1.call-done = f32[128,768]{1,0:T(8,128)} async-done(((f32[128,12288]{1,0:T(8,128)}), f32[128,768]{1,0:T(8,128)}) %reduce-scatter.5.cloned.1.call-update) | async-done | bytes 393232 | tf_op jit(solution)/shard_map/reduce_scatter | solution.py:42
  663.6 65.7 %psum.29 = f32[64,64]{0,1:T(8,128)S(1)} all-reduce(f32[64,64]{0,1:T(8,128)S(1)} %convolution_multiply_fusion.2), channel_id=1, replica_groups=mesh['row'=8,'col'=16] {'row','col'}, use_global_device_ids=true, to_apply=%region_9.10 | all-reduce | flops 4096 | bytes 32768 | tf_op jit(solution)/shard_map/psum | solution.py:76
  730.4 14.3 %all_gather.14 = bf16[64,6144]{1,0:T(8,128)(2,1)S(1)} all-gather(bf16[64,768]{1,0:T(8,128)(2,1)} %get-tuple-element.250), channel_id=1, replica_groups=mesh['row'=8,'col'=16] {'row'}, dimensions={1}, use_global_device_ids=true | all-gather | bytes 884736 | tf_op jit(solution)/shard_map/all_gather | solution.py:12
  745.8 24.0 %all-gather.8.cloned.1.call-done = bf16[64,12288]{1,0:T(8,128)(2,1)} async-done(((bf16[64,768]{1,0:T(8,128)(2,1)}), bf16[64,12288]{1,0:T(8,128)(2,1)}) %all-gather.8.cloned.1.call-update) | async-done | bytes 1572880 | tf_op jit(solution)/shard_map/all_gather | solution.py:11
  776.2 198.4 %while.27 = (s32[]{:T(128)}, f32[64,96,128]{2,0,1:T(8,128)}, f32[64,48,128]{2,0,1:T(8,128)}, s32[]{:T(128)}, s32[576]{0:T(1024)S(1)}, /*index=5*/s32[]{:T(128)},...) while((s32[]{:T(128)}, f32[64,96,128]{2,0,1:T(8,128)}, ...), condition=%wide.region_13.14_spmd.clone, body=%wide.region_10.13_spmd.clone.sunk | while | flops 272632704 | bytes 27274384 | solution.py:41
  782.0 9.0 scatter_fusion.2
  795.5 9.0 scatter_fusion.3
  838.7 9.0 scatter_fusion.2
  923.6 9.1 scatter_fusion.2
  981.7 80.2 %reduce-scatter.11.cloned.1.call-done = f32[64,768]{1,0:T(8,128)} async-done(((f32[64,6144]{1,0:T(8,128)}), f32[64,768]{1,0:T(8,128)}) %reduce-scatter.11.cloned.1.call-update) | async-done | bytes 196624 | tf_op jit(solution)/shard_map/reduce_scatter | solution.py:45
  1061.9 79.4 %reduce-scatter.9.cloned.1.call-done = f32[64,768]{1,0:T(8,128)} async-done(((f32[64,12288]{1,0:T(8,128)}), f32[64,768]{1,0:T(8,128)}) %reduce-scatter.9.cloned.1.call-update) | async-done | bytes 196624 | tf_op jit(solution)/shard_map/reduce_scatter | solution.py:42
  1143.7 148.1 %all-reduce.3.cloned.1.call-done = (f32[192,192]{1,0:T(8,128)}, f32[192,192]{1,0:T(8,128)}) async-done(((f32[192,192]{1,0:T(8,128)}, f32[192,192]{1,0:T(8,128)}), (f32[192,192]{1,0:T(8,128)}, f32[192,192]{1,0:T(8,128)})) %all-reduce.3.cloned.1.call-update) | async-done | bytes 294928 | tf_op jit(solution)/shard_map/psum | solution.py:84
  (199 shorter events, 415.5 us)
Async XLA Ops:
  7.2 0.9 copy-start
  7.2 85.8 %copy-start.8 = (s32[1,1,576]{2,1,0:T(1,128)S(1)}, s32[1,1,576]{2,1,0:T(1,128)}, u32[]{:S(2)}) copy-start(s32[1,1,576]{2,1,0:T(1,128)} %param.12) | copy-start | bytes 6916
  7.2 85.8 %copy-start.9 = (s32[1,1,576]{2,1,0:T(1,128)S(1)}, s32[1,1,576]{2,1,0:T(1,128)}, u32[]{:S(2)}) copy-start(s32[1,1,576]{2,1,0:T(1,128)} %param.13) | copy-start | bytes 6916
  7.2 105.7 %all-gather.4.cloned.1.call-start = ((), (), s32[]{:S(2)}) async-start(), calls=%async_computation.4 | async-start | bytes 1769472 | tf_op jit(solution)/shard_map/all_gather | solution.py:12
  91.5 71.8 %all-gather.6.cloned.1.call-start = ((), (), s32[]{:S(2)}) async-start(), calls=%async_computation.5 | async-start | bytes 3342336 | tf_op jit(solution)/shard_map/all_gather | solution.py:11
  92.3 484.5 %reduce-scatter.7.cloned.1.call-start = ((), (), s32[]{:S(2)}) async-start(), calls=%async_computation.7 | async-start | bytes 3538944 | tf_op jit(solution)/shard_map/reduce_scatter | solution.py:45
  464.2 198.0 %reduce-scatter.5.cloned.1.call-start = ((), (), s32[]{:S(2)}) async-start(), calls=%async_computation.6 | async-start | bytes 6684672 | tf_op jit(solution)/shard_map/reduce_scatter | solution.py:42
  470.3 299.4 %all-gather.8.cloned.1.call-start = ((), (), s32[]{:S(2)}) async-start(), calls=%async_computation.8 | async-start | bytes 1671168 | tf_op jit(solution)/shard_map/all_gather | solution.py:11
  663.3 109.5 %copy-start.3 = (f32[128,768]{1,0:T(8,128)}, f32[128,768]{1,0:T(8,128)S(1)}, u32[]{:S(2)}) copy-start(f32[128,768]{1,0:T(8,128)S(1)} %add.116) | copy-start | bytes 1179652
  730.3 331.6 %reduce-scatter.11.cloned.1.call-start = ((), (), s32[]{:S(2)}) async-start(), calls=%async_computation.10 | async-start | bytes 1769472 | tf_op jit(solution)/shard_map/reduce_scatter | solution.py:45
  974.6 2.9 copy-start.2
  977.4 163.9 %reduce-scatter.9.cloned.1.call-start = ((), (), s32[]{:S(2)}) async-start(), calls=%async_computation.9 | async-start | bytes 3342336 | tf_op jit(solution)/shard_map/reduce_scatter | solution.py:42
  979.3 0.9 copy-start.5
  979.3 1.0 copy-start.6
  979.3 2.3 copy-start.4
  979.3 312.4 %all-reduce.3.cloned.1.call-start = ((), (), s32[]{:S(2)}) async-start(), calls=%async_computation.11 | async-start | bytes 786432 | tf_op jit(solution)/shard_map/psum | solution.py:84
  980.3 314.7 %copy-start.1 = (f32[64,768]{1,0:T(8,128)S(1)}, f32[64,768]{1,0:T(8,128)}, u32[]{:S(2)}) copy-start(f32[64,768]{1,0:T(8,128)} %param.10) | copy-start | bytes 589828
  1142.3 152.7 %copy-start.7 = (f32[64,768]{1,0:T(8,128)}, f32[64,768]{1,0:T(8,128)S(1)}, u32[]{:S(2)}) copy-start(f32[64,768]{1,0:T(8,128)S(1)} %add.117) | copy-start | bytes 589828
Sparse Core Ops, SparseCore 0:
  91.7 21.1 all-gather.3
  115.6 47.6 all-gather.5
  464.3 112.4 reduce-scatter.6
  580.0 82.0 reduce-scatter.4
  730.4 39.2 all-gather.7
  977.5 84.3 reduce-scatter.10
  1065.2 76.0 reduce-scatter.8
  1146.6 145.1 all-reduce.2
where the time goes:
time: 1310 us; the launch traced here: 1300 us
  waiting for transfers between devices  591 us (45%)
  other arithmetic  309 us (24%)
  blocking collectives  149 us (11%)
  local copies, waits for them, and re-layouts  118 us (9%)
  matrix products  118 us (9%)
  between operations  15 us (1%)
    reduce_scatter x2, waiting for transfers between devices, apply_graph(): lax.psum_scatter(col_totals.reshape(vec_width, -1), 'row', scatter_dimens...  187 us
    reduce_scatter x2, waiting for transfers between devices, apply_graph(): lax.psum_scatter(row_totals.reshape(vec_width, -1), 'col', scatter_dimens...  165 us
    scatter-add x14, other arithmetic, turn(): row_totals.at[:, row_index].add(forward)  158 us
    psum x1, waiting for transfers between devices, per_device(): lax.psum((product(basis, images), product(basis, basis)), ('row', 'col'))  148 us
    scatter-add x14, other arithmetic, turn(): col_totals.at[:, col_index].add(backward)  125 us
    all_gather x2, waiting for transfers between devices, apply_graph(): row_range = lax.all_gather(vectors, 'col', axis=1, tiled=True)  71.4 us
    psum x1, blocking collectives, per_device(): gram_x = lax.psum(product(block_x, block_x), ('row', 'col'))  68.9 us
    psum x1, blocking collectives, per_device(): rayleigh = lax.psum(product(orthonormal, image_x), ('row', 'col'))  65.7 us
  transfers between devices with their start and end apart: 8, of which 8 were waited for; matrix products, arithmetic and copies ran while one was open for 1% of the time, Pallas kernels for 0%

commit v1 on v0

--- a/solution.py
+++ b/solution.py
@@ -1,8 +1,18 @@
+import functools
 import math
 import jax
 import jax.numpy as jnp
 from jax import lax
 from jax.sharding import PartitionSpec as P
+
+
+def lanes_settle(z, ax_name, dev_axis):
+    for no in (ax_name, dev_axis):
+        z = jax.lax.psum(z, axis_name=no)
+    return z
+
+
+_end_regions = functools.partial(lanes_settle, ax_name="col", dev_axis="row")
 
 
 def apply_graph(vectors, tile_rows, tile_cols, live_count, tile_vals):
@@ -81,7 +91,7 @@
     image_r = apply_graph(residual_low, slot_rows, slot_cols, live_count, slot_vals)
     basis = jnp.concatenate([orthonormal, residual, block_p], axis=0)
     images = jnp.concatenate([image_x, image_r, image_p], axis=0)
-    gram_a, gram_b = lax.psum((product(basis, images), product(basis, basis)), ("row", "col"))
+    gram_a, gram_b = _end_regions((product(basis, images), product(basis, basis)))
     return (residual, image_r, gram_a, gram_b)
 
 

time: 1310 us -> 1330 us (1.015)
  other arithmetic: 309 us -> 325 us
    and x14, other arithmetic: 1.14 us -> 14.6 us  [turn(): row_inputs = jnp.take(row_blocks, row_index, axis=1)]
    psum x1 -> x2, waiting for transfers between devices: 148 us -> 146 us  [lanes_settle(): z = jax.lax.psum(z, axis_name=no)]
  transfers between devices with their start and end apart: 8 -> 9, of which waited for: 8 -> 9; matrix products, arithmetic and copies ran while one was open for 1% -> 1% of each run, Pallas kernels for 0% -> 0%
where the time goes in v1:
time: 1330 us; the launch traced here: 1320 us
  waiting for transfers between devices  593 us (45%)
  other arithmetic  325 us (24%)
  blocking collectives  149 us (11%)
  matrix products  119 us (9%)
  local copies, waits for them, and re-layouts  118 us (9%)
  between operations  14.7 us (1%)
    reduce_scatter x2, waiting for transfers between devices, apply_graph(): lax.psum_scatter(col_totals.reshape(vec_width, -1), 'row', scatter_dimens...  191 us
    reduce_scatter x2, waiting for transfers between devices, apply_graph(): lax.psum_scatter(row_totals.reshape(vec_width, -1), 'col', scatter_dimens...  165 us
    scatter-add x14, other arithmetic, turn(): row_totals.at[:, row_index].add(forward)  160 us
    psum x2, waiting for transfers between devices, lanes_settle(): z = jax.lax.psum(z, axis_name=no)  146 us
    scatter-add x14, other arithmetic, turn(): col_totals.at[:, col_index].add(backward)  125 us
    all_gather x2, waiting for transfers between devices, apply_graph(): row_range = lax.all_gather(vectors, 'col', axis=1, tiled=True)  71.3 us
    psum x1, blocking collectives, per_device(): gram_x = lax.psum(product(block_x, block_x), ('row', 'col'))  68.9 us
    psum x1, blocking collectives, per_device(): rayleigh = lax.psum(product(orthonormal, image_x), ('row', 'col'))  65.7 us
  transfers between devices with their start and end apart: 9, of which 9 were waited for; matrix products, arithmetic and copies ran while one was open for 1% of the time, Pallas kernels for 0%

profile of v1, /device:TPU:1, one launch (start us, length us, event | category | flops | bytes accessed | tf_op | source)
XLA Modules:
  0.0 1320.4 jit_solution(5548266342379263663)
XLA Ops:
  8.4 68.9 %psum.42 = f32[64,64]{0,1:T(8,128)S(1)} all-reduce(f32[64,64]{0,1:T(8,128)S(1)} %convolution_multiply_fusion.3), channel_id=1, replica_groups=mesh['row'=8,'col'=16] {'row','col'}, use_global_device_ids=true, to_apply=%region_0.0 | all-reduce | flops 4096 | bytes 32768 | tf_op jit(solution)/shard_map/psum | solution.py:76
  93.6 19.2 %all-gather.4.cloned.1.call-done = bf16[128,6144]{1,0:T(8,128)(2,1)} async-done(((bf16[128,768]{1,0:T(8,128)(2,1)}), bf16[128,6144]{1,0:T(8,128)(2,1)}) %all-gather.4.cloned.1.call-update) | async-done | bytes 1572880 | tf_op jit(solution)/shard_map/all_gather | solution.py:22
  115.8 47.5 %all-gather.6.cloned.1.call-done = bf16[128,12288]{1,0:T(8,128)(2,1)} async-done(((bf16[128,768]{1,0:T(8,128)(2,1)}), bf16[128,12288]{1,0:T(8,128)(2,1)}) %all-gather.6.cloned.1.call-update) | async-done | bytes 3145744 | tf_op jit(solution)/shard_map/all_gather | solution.py:21
  171.6 295.8 %while.26 = (s32[]{:T(128)}, f32[128,96,128]{2,0,1:T(8,128)}, f32[128,48,128]{2,0,1:T(8,128)S(1)}, s32[]{:T(128)}, s32[576]{0:T(1024)S(1)}, /*index=5*/s32[]{:T(...) while((s32[]{:T(128)}, f32[128,96,128]{2,0,1:T(8,128)}, ...), condition=%wide.region_6.7_spmd.clone, body=%wide.region_3.6_spmd.clone.sunk | while | flops 543165312 | bytes 50343056 | solution.py:51
  182.4 13.7 %scatter_fusion = f32[128,96,128]{2,0,1:T(8,128)} fusion(f32[128,96,128]{2,0,1:T(8,128)} %get-tuple-element.409, s32[64]{0:T(128)S(1)} %get-tuple-element.376, f32[64,128,128]{2,1,0:T(8,128)} %fusion.80), kind=kCustom, calls=%fused_computation.4.clone.clone.1 | custom fusion | flops 1048576 | bytes 12583168 | tf_op jit(solution)/shard_map/while/body/scatter-add | solution.py:47
  224.6 13.7 %scatter_fusion = f32[128,96,128]{2,0,1:T(8,128)} fusion(f32[128,96,128]{2,0,1:T(8,128)} %get-tuple-element.409, s32[64]{0:T(128)S(1)} %get-tuple-element.376, f32[64,128,128]{2,1,0:T(8,128)} %fusion.80), kind=kCustom, calls=%fused_computation.4.clone.clone.1 | custom fusion | flops 1048576 | bytes 12583168 | tf_op jit(solution)/shard_map/while/body/scatter-add | solution.py:47
  266.9 13.7 %scatter_fusion = f32[128,96,128]{2,0,1:T(8,128)} fusion(f32[128,96,128]{2,0,1:T(8,128)} %get-tuple-element.409, s32[64]{0:T(128)S(1)} %get-tuple-element.376, f32[64,128,128]{2,1,0:T(8,128)} %fusion.80), kind=kCustom, calls=%fused_computation.4.clone.clone.1 | custom fusion | flops 1048576 | bytes 12583168 | tf_op jit(solution)/shard_map/while/body/scatter-add | solution.py:47
  309.1 13.6 %scatter_fusion = f32[128,96,128]{2,0,1:T(8,128)} fusion(f32[128,96,128]{2,0,1:T(8,128)} %get-tuple-element.409, s32[64]{0:T(128)S(1)} %get-tuple-element.376, f32[64,128,128]{2,1,0:T(8,128)} %fusion.80), kind=kCustom, calls=%fused_computation.4.clone.clone.1 | custom fusion | flops 1048576 | bytes 12583168 | tf_op jit(solution)/shard_map/while/body/scatter-add | solution.py:47
  351.3 13.8 %scatter_fusion = f32[128,96,128]{2,0,1:T(8,128)} fusion(f32[128,96,128]{2,0,1:T(8,128)} %get-tuple-element.409, s32[64]{0:T(128)S(1)} %get-tuple-element.376, f32[64,128,128]{2,1,0:T(8,128)} %fusion.80), kind=kCustom, calls=%fused_computation.4.clone.clone.1 | custom fusion | flops 1048576 | bytes 12583168 | tf_op jit(solution)/shard_map/while/body/scatter-add | solution.py:47
  393.7 13.7 %scatter_fusion = f32[128,96,128]{2,0,1:T(8,128)} fusion(f32[128,96,128]{2,0,1:T(8,128)} %get-tuple-element.409, s32[64]{0:T(128)S(1)} %get-tuple-element.376, f32[64,128,128]{2,1,0:T(8,128)} %fusion.80), kind=kCustom, calls=%fused_computation.4.clone.clone.1 | custom fusion | flops 1048576 | bytes 12583168 | tf_op jit(solution)/shard_map/while/body/scatter-add | solution.py:47
  435.9 13.7 %scatter_fusion = f32[128,96,128]{2,0,1:T(8,128)} fusion(f32[128,96,128]{2,0,1:T(8,128)} %get-tuple-element.409, s32[64]{0:T(128)S(1)} %get-tuple-element.376, f32[64,128,128]{2,1,0:T(8,128)} %fusion.80), kind=kCustom, calls=%fused_computation.4.clone.clone.1 | custom fusion | flops 1048576 | bytes 12583168 | tf_op jit(solution)/shard_map/while/body/scatter-add | solution.py:47
  475.5 107.7 %reduce-scatter.7.cloned.1.call-done = f32[128,768]{1,0:T(8,128)} async-done(((f32[128,6144]{1,0:T(8,128)}), f32[128,768]{1,0:T(8,128)}) %reduce-scatter.7.cloned.1.call-update) | async-done | bytes 393232 | tf_op jit(solution)/shard_map/reduce_scatter | solution.py:55
  583.2 85.6 %reduce-scatter.5.cloned.1.call-done = f32[128,768]{1,0:T(8,128)} async-done(((f32[128,12288]{1,0:T(8,128)}), f32[128,768]{1,0:T(8,128)}) %reduce-scatter.5.cloned.1.call-update) | async-done | bytes 393232 | tf_op jit(solution)/shard_map/reduce_scatter | solution.py:52
  670.3 65.7 %psum.43 = f32[64,64]{0,1:T(8,128)S(1)} all-reduce(f32[64,64]{0,1:T(8,128)S(1)} %convolution_multiply_fusion.2), channel_id=1, replica_groups=mesh['row'=8,'col'=16] {'row','col'}, use_global_device_ids=true, to_apply=%region_9.10 | all-reduce | flops 4096 | bytes 32768 | tf_op jit(solution)/shard_map/psum | solution.py:86
  737.0 14.5 %all_gather.14 = bf16[64,6144]{1,0:T(8,128)(2,1)S(1)} all-gather(bf16[64,768]{1,0:T(8,128)(2,1)} %get-tuple-element.252), channel_id=1, replica_groups=mesh['row'=8,'col'=16] {'row'}, dimensions={1}, use_global_device_ids=true | all-gather | bytes 884736 | tf_op jit(solution)/shard_map/all_gather | solution.py:22
  752.6 23.9 %all-gather.8.cloned.1.call-done = bf16[64,12288]{1,0:T(8,128)(2,1)} async-done(((bf16[64,768]{1,0:T(8,128)(2,1)}), bf16[64,12288]{1,0:T(8,128)(2,1)}) %all-gather.8.cloned.1.call-update) | async-done | bytes 1572880 | tf_op jit(solution)/shard_map/all_gather | solution.py:21
  782.8 208.8 %while.27 = (s32[]{:T(128)}, f32[64,96,128]{2,0,1:T(8,128)}, f32[64,48,128]{2,0,1:T(8,128)}, s32[]{:T(128)}, s32[576]{0:T(1024)S(1)}, /*index=5*/s32[]{:T(128)},...) while((s32[]{:T(128)}, f32[64,96,128]{2,0,1:T(8,128)}, ...), condition=%wide.region_13.14_spmd.clone, body=%wide.region_10.13_spmd.clone.sunk | while | flops 272632704 | bytes 27293320 | solution.py:51
  819.7 9.2 scatter_fusion.2
  833.4 9.2 scatter_fusion.3
  863.4 9.2 scatter_fusion.3
  998.7 83.6 %reduce-scatter.11.cloned.1.call-done = f32[64,768]{1,0:T(8,128)} async-done(((f32[64,6144]{1,0:T(8,128)}), f32[64,768]{1,0:T(8,128)}) %reduce-scatter.11.cloned.1.call-update) | async-done | bytes 196624 | tf_op jit(solution)/shard_map/reduce_scatter | solution.py:55
  1082.3 79.0 %reduce-scatter.9.cloned.1.call-done = f32[64,768]{1,0:T(8,128)} async-done(((f32[64,12288]{1,0:T(8,128)}), f32[64,768]{1,0:T(8,128)}) %reduce-scatter.9.cloned.1.call-update) | async-done | bytes 196624 | tf_op jit(solution)/shard_map/reduce_scatter | solution.py:52
  1164.8 84.4 %all-reduce.5.cloned.1.call-done = (f32[192,192]{1,0:T(8,128)}, f32[192,192]{1,0:T(8,128)}) async-done(((f32[192,192]{1,0:T(8,128)}, f32[192,192]{1,0:T(8,128)}), (f32[192,192]{1,0:T(8,128)}, f32[192,192]{1,0:T(8,128)})) %all-reduce.5.cloned.1.call-update) | async-done | bytes 294928 | tf_op jit(solution)/shard_map/psum | solution.py:11
  1249.2 61.4 %all-reduce.7.cloned.1.call-done = (f32[192,192]{1,0:T(8,128)}, f32[192,192]{1,0:T(8,128)}) async-done(((f32[192,192]{1,0:T(8,128)}, f32[192,192]{1,0:T(8,128)}), (f32[192,192]{1,0:T(8,128)}, f32[192,192]{1,0:T(8,128)})) %all-reduce.7.cloned.1.call-update) | async-done | bytes 294928 | tf_op jit(solution)/shard_map/psum | solution.py:11
  (230 shorter events, 440.5 us)
Async XLA Ops:
  7.2 85.8 %copy-start.10 = (s32[1,1,576]{2,1,0:T(1,128)S(1)}, s32[1,1,576]{2,1,0:T(1,128)}, u32[]{:S(2)}) copy-start(s32[1,1,576]{2,1,0:T(1,128)} %param.12) | copy-start | bytes 6916
  7.2 85.8 %copy-start.11 = (s32[1,1,576]{2,1,0:T(1,128)S(1)}, s32[1,1,576]{2,1,0:T(1,128)}, u32[]{:S(2)}) copy-start(s32[1,1,576]{2,1,0:T(1,128)} %param.13) | copy-start | bytes 6916
  7.2 105.7 %all-gather.4.cloned.1.call-start = ((), (), s32[]{:S(2)}) async-start(), calls=%async_computation.4 | async-start | bytes 1769472 | tf_op jit(solution)/shard_map/all_gather | solution.py:22
  91.5 71.8 %all-gather.6.cloned.1.call-start = ((), (), s32[]{:S(2)}) async-start(), calls=%async_computation.5 | async-start | bytes 3342336 | tf_op jit(solution)/shard_map/all_gather | solution.py:21
  92.3 490.9 %reduce-scatter.7.cloned.1.call-start = ((), (), s32[]{:S(2)}) async-start(), calls=%async_computation.7 | async-start | bytes 3538944 | tf_op jit(solution)/shard_map/reduce_scatter | solution.py:55
  469.3 199.5 %reduce-scatter.5.cloned.1.call-start = ((), (), s32[]{:S(2)}) async-start(), calls=%async_computation.6 | async-start | bytes 6684672 | tf_op jit(solution)/shard_map/reduce_scatter | solution.py:52
  475.5 301.0 %all-gather.8.cloned.1.call-start = ((), (), s32[]{:S(2)}) async-start(), calls=%async_computation.8 | async-start | bytes 1671168 | tf_op jit(solution)/shard_map/all_gather | solution.py:21
  670.0 109.5 %copy-start.3 = (f32[128,768]{1,0:T(8,128)}, f32[128,768]{1,0:T(8,128)S(1)}, u32[]{:S(2)}) copy-start(f32[128,768]{1,0:T(8,128)S(1)} %add.120) | copy-start | bytes 1179652
  736.9 259.6 %copy-start.6 = (f32[64,768]{1,0:T(8,128)}, f32[64,768]{1,0:T(8,128)S(1)}, u32[]{:S(2)}) copy-start(f32[64,768]{1,0:T(8,128)S(1)} %get-tuple-element.478) | copy-start | bytes 589828
  737.0 345.4 %reduce-scatter.11.cloned.1.call-start = ((), (), s32[]{:S(2)}) async-start(), calls=%async_computation.10 | async-start | bytes 1769472 | tf_op jit(solution)/shard_map/reduce_scatter | solution.py:55
  803.5 9.2 copy-start.9
  833.4 9.2 copy-start.9
  863.4 9.2 copy-start.9
  872.5 3.2 copy-start.8
  893.2 9.1 copy-start.9
  902.4 3.2 copy-start.8
  923.0 9.1 copy-start.9
  952.8 9.1 copy-start.9
  982.6 9.1 copy-start.9
  994.5 166.8 %reduce-scatter.9.cloned.1.call-start = ((), (), s32[]{:S(2)}) async-start(), calls=%async_computation.9 | async-start | bytes 3342336 | tf_op jit(solution)/shard_map/reduce_scatter | solution.py:52
  996.5 252.7 %all-reduce.5.cloned.1.call-start = ((), (), s32[]{:S(2)}) async-start(), calls=%async_computation.11 | async-start | bytes 786432 | tf_op jit(solution)/shard_map/psum | solution.py:11
  998.7 315.2 %copy-start.1 = (f32[64,768]{1,0:T(8,128)S(1)}, f32[64,768]{1,0:T(8,128)}, u32[]{:S(2)}) copy-start(f32[64,768]{1,0:T(8,128)} %param.10) | copy-start | bytes 589828
  1162.4 151.5 %copy-start.7 = (f32[64,768]{1,0:T(8,128)}, f32[64,768]{1,0:T(8,128)S(1)}, u32[]{:S(2)}) copy-start(f32[64,768]{1,0:T(8,128)S(1)} %add.121) | copy-start | bytes 589828
  1164.8 145.9 %all-reduce.7.cloned.1.call-start = ((), (), s32[]{:S(2)}) async-start(), calls=%async_computation.12 | async-start | bytes 786432 | tf_op jit(solution)/shard_map/psum | solution.py:11
  (9 other events, 23.1 us)
Sparse Core Ops, SparseCore 0:
  91.7 21.1 all-gather.3
  115.6 47.6 all-gather.5
  469.5 113.6 reduce-scatter.6
  586.5 82.2 reduce-scatter.4
  737.1 39.3 all-gather.7
  994.6 87.6 reduce-scatter.10
  1085.6 75.6 reduce-scatter.8
  1165.2 83.9 all-reduce.4
  1251.6 58.9 all-reduce.6
